TPU v7x, 32 devices: a whole 2x2x4 slice. The times are simulated.
32 devices in a mesh: tm: 8 (over z, core), freq: 4 (over y, x).
Axes of the slice: x: 2, y: 2, z: 4, core: 2. Of those that a mesh axis runs over, the one named last changes fastest.
Arguments:
- tokens: bfloat16 [128, 64, 1024], P('tm', 'freq'), may hold values from -16 to 16
- w_query: bfloat16 [1024, 1024], replicated, may hold values from -1 to 1
- w_key: bfloat16 [1024, 1024], replicated, may hold values from -1 to 1
- w_value: bfloat16 [1024, 1024], replicated, may hold values from -0.1875 to 0.1875
- w_out: bfloat16 [1024, 1024], replicated, may hold values from -0.75 to 0.75
- d_out: bfloat16 [128, 64, 1024], P('tm', 'freq'), may hold values from -6 to 6
Outputs:
- output: bfloat16 [128, 64, 1024], P('tm', 'freq')
- input_grad: bfloat16 [128, 64, 1024], P('tm', 'freq')
- weight_grads: float32 [1024, 4, 1024], P(('tm', 'freq'))
All inputs are finite; a program needn't handle non-finite values.
Results may differ from a plain program's by a relative error of at most 0.0093.
Values may be sent and summed in bfloat16 or wider, within the bound.
A program may use at most 256 MiB of HBM per device.

v0:
```python
import functools
import math

import jax
import jax.numpy as jnp
from jax import lax
from jax.experimental import pallas as pl
from jax.experimental.pallas import tpu as pltpu
from jax.sharding import PartitionSpec as P

HEADS = 8
REACH = 6
EPS = 1e-05
FAR = -1e30
MESH = pl.DeviceIdType.MESH
F32 = jnp.float32
BF16 = jnp.bfloat16


def nn(a, b):
    return lax.dot_general(a, b, (((1,), (0,)), ((), ())), preferred_element_type=F32)


def nt(a, b):
    return lax.dot_general(a, b, (((1,), (1,)), ((), ())), preferred_element_type=F32)


def query_kernel(scale, lay, *refs):
    q_ref, g_ref, k_ref, v_ref, bias_ref, grad, grad_s, grad_c = refs[:8]
    att_ref, gq_ref, stat_ref, far_ref, near, s_sem, r_sem = refs[8:]
    h = pl.program_id(0)
    n_q = lay.own // 2
    ex = Exchange(lay, near, edge_source(lay, grad, grad_s, grad_c), s_sem, r_sem)

    @pl.when(h == 0)
    def _():
        ex.nb.greet()
        ex.start()
        ex.clear()
        stat_ref[...] = jnp.zeros(stat_ref.shape, F32)

    for half in range(2):
        out = slice(half * n_q, (half + 1) * n_q)
        rows = slice(lay.start + half * n_q, lay.start + (half + 1) * n_q)
        cols = lay.reach(half)
        k = k_ref[cols, :]
        v = v_ref[cols, :]
        s = nt(q_ref[rows, :], k) * scale + bias_ref[half]
        top = jnp.max(s, axis=-1, keepdims=True)
        e = jnp.exp(s - top)
        total = jnp.sum(e, axis=-1, keepdims=True)
        probs = e * (1.0 / total)
        att_ref[out, :] = nn(probs.astype(BF16), v).astype(BF16)
        gp = nt(g_ref[out, :], v)
        spread = jnp.sum(probs * gp, axis=-1, keepdims=True)
        gs = (probs * (gp - spread) * scale).astype(BF16)
        gq_ref[out, :] = nn(gs, k).astype(BF16)
        lane = lax.broadcasted_iota(jnp.int32, (n_q, 128), 1)
        kept = jnp.where(lane == 2 * h + 1, spread, stat_ref[out, :])
        stat_ref[out, :] = jnp.where(lane == 2 * h, top + jnp.log(total), kept)

    @pl.when(h == HEADS - 1)
    def _():
        ex.arrive()
        far_ref[: lay.start, :] = near[: lay.start, :]
        far_ref[lay.start : lay.start + lay.own, :] = jnp.zeros((lay.own, near.shape[1]), BF16)
        far_ref[lay.start + lay.own :, :] = near[lay.start + lay.own :, :]
        ex.sent()


def key_kernel(scale, lay, k_ref, v_ref, q_ref, g_ref, bias_ref, stat_ref, gk_ref, gv_ref):
    h = pl.program_id(0)
    n_q = lay.own // 2
    for half in range(2):
        out = slice(half * n_q, (half + 1) * n_q)
        rows = slice(lay.start + half * n_q, lay.start + (half + 1) * n_q)
        cols = lay.reach(half)
        q = q_ref[cols, :]
        g = g_ref[cols, :]
        s = nt(k_ref[rows, :], q) * scale + bias_ref[half]
        probs = jnp.exp(s - stat_ref[half, pl.ds(2 * h, 1), :])
        gv_ref[out, :] = nn(probs.astype(BF16), g).astype(BF16)
        gp = nt(v_ref[rows, :], g)
        gs = (probs * (gp - stat_ref[half, pl.ds(2 * h + 1, 1), :]) * scale).astype(BF16)
        gk_ref[out, :] = nn(gs, q).astype(BF16)


def attention_calls(lay, width, model):
    scale = 1.0 / math.sqrt(width)
    own = pl.BlockSpec((lay.own, width), lambda h: (0, h))
    ext = pl.BlockSpec((lay.all, width), lambda h: (0, h))
    bias = pl.BlockSpec((2, lay.own // 2, lay.span), lambda h: (0, 0, 0))
    big = jax.ShapeDtypeStruct((lay.own, model), BF16)
    params = pltpu.CompilerParams(vmem_limit_bytes=32 * 1024 * 1024)
    first = pl.pallas_call(
        functools.partial(query_kernel, scale, lay),
        grid=(HEADS,),
        in_specs=[ext, own, ext, ext, bias] + [pl.BlockSpec(memory_space=pl.ANY)] * 3,
        out_specs=[
            own,
            own,
            pl.BlockSpec((lay.own, 128), lambda h: (0, 0)),
            pl.BlockSpec((lay.all, model), lambda h: (0, 0)),
        ],
        out_shape=[
            big,
            big,
            jax.ShapeDtypeStruct((lay.own, 128), F32),
            jax.ShapeDtypeStruct((lay.all, model), BF16),
        ],
        scratch_shapes=[pltpu.VMEM((lay.all, model), BF16)] + [pltpu.SemaphoreType.DMA((len(SIDES),))] * 2,
        compiler_params=pltpu.CompilerParams(
            collective_id=4, has_side_effects=True, vmem_limit_bytes=32 * 1024 * 1024
        ),
    )
    second = pl.pallas_call(
        functools.partial(key_kernel, scale, lay),
        grid=(HEADS,),
        in_specs=[ext, ext, ext, ext, bias, pl.BlockSpec((2, 128, lay.span), lambda h: (0, 0, 0))],
        out_specs=[own, own],
        out_shape=[big, big],
        compiler_params=params,
    )
    return first, second


SIDES = ((0, 1), (0, -1), (1, 0), (-1, 0), (1, 1), (1, -1), (-1, 1), (-1, -1))


class Layout:
    def __init__(self, n_t, n_f):
        self.n_t, self.n_f = n_t, n_f
        self.own = n_t * n_f
        corner = -(-REACH * REACH // 16) * 16
        self.corner = corner
        sizes = {
            (-1, -1): corner,
            (-1, 1): corner,
            (-1, 0): REACH * n_f,
            (0, 0): self.own,
            (0, -1): REACH * n_t,
            (0, 1): REACH * n_t,
            (1, 0): REACH * n_f,
            (1, -1): corner,
            (1, 1): corner,
        }
        self.size = sizes
        self.at = {}
        self.all = 0
        for side, size in sizes.items():
            self.at[side] = self.all
            self.all += size
        self.start = self.at[0, 0]
        self.span = self.at[1, 0]

    def reach(self, half):
        return slice(0, self.span) if half == 0 else slice(self.start, self.all)

    def region(self, side):
        return slice(self.at[side], self.at[side] + self.size[side])

    def place(self, index):
        far = 1 << 20
        time = jnp.full(index.shape, far, jnp.int32)
        freq = jnp.full(index.shape, far, jnp.int32)
        for (dt, df), size in self.size.items():
            r = index - self.at[dt, df]
            n_col = self.n_f if df == 0 else REACH
            n_row = self.n_t if dt == 0 else REACH
            here = (r >= 0) & (r < n_row * n_col)
            t0 = 0 if dt == 0 else (-REACH if dt < 0 else self.n_t)
            f0 = 0 if df == 0 else (-REACH if df < 0 else self.n_f)
            time = jnp.where(here, t0 + r // n_col, time)
            freq = jnp.where(here, f0 + r % n_col, freq)
        return time, freq


def window_bias(lay):
    t0 = lax.axis_index("tm") * lay.n_t
    f0 = lax.axis_index("freq") * lay.n_f
    parts = []
    for half in range(2):
        own = half * (lay.own // 2) + jnp.arange(lay.own // 2)[:, None]
        cols = lay.reach(half)
        key_t, key_f = lay.place(jnp.arange(cols.start, cols.stop))
        inside = (
            (t0 + key_t >= 0)
            & (t0 + key_t < lay.n_t * lax.axis_size("tm"))
            & (f0 + key_f >= 0)
            & (f0 + key_f < lay.n_f * lax.axis_size("freq"))
        )
        ok = (
            (jnp.abs(key_t[None] - own // lay.n_f) <= REACH)
            & (jnp.abs(key_f[None] - own % lay.n_f) <= REACH)
            & inside[None]
        )
        parts.append(jnp.where(ok, 0.0, FAR).astype(F32))
    return jnp.stack(parts)


def opposite(side):
    return (-side[0], -side[1])


class Neighbours:
    def __init__(self):
        self.tm, self.fq = lax.axis_index("tm"), lax.axis_index("freq")
        self.t_size, self.f_size = lax.axis_size("tm"), lax.axis_size("freq")

    def exists(self, side):
        t, f = self.tm + side[0], self.fq + side[1]
        return (t >= 0) & (t < self.t_size) & (f >= 0) & (f < self.f_size)

    def device(self, side):
        return ((self.tm + side[0] + self.t_size) % self.t_size, (self.fq + side[1] + self.f_size) % self.f_size)

    def greet(self):
        barrier = pltpu.get_barrier_semaphore()
        for side in SIDES:

            @pl.when(self.exists(side))
            def _(side=side):
                pl.semaphore_signal(barrier, inc=1, device_id=self.device(side), device_id_type=MESH)

        pl.semaphore_wait(barrier, sum(self.exists(side).astype(jnp.int32) for side in SIDES))


class Exchange:
    def __init__(self, lay, near, source, send_sem, recv_sem):
        self.near, self.lay, self.nb = near, lay, Neighbours()
        self.source, self.send_sem, self.recv_sem = source, send_sem, recv_sem

    def copy(self, i):
        side = SIDES[i]
        to = self.lay.region(opposite(side))
        return pltpu.make_async_remote_copy(
            src_ref=self.source(side),
            dst_ref=self.near.at[pl.ds(to.start, to.stop - to.start)],
            send_sem=self.send_sem.at[i],
            recv_sem=self.recv_sem.at[i],
            device_id=self.nb.device(side),
            device_id_type=MESH,
        )

    def start(self):
        for i, side in enumerate(SIDES):

            @pl.when(self.nb.exists(side))
            def _(i=i):
                self.copy(i).start()

    def clear(self):
        for side in SIDES:

            @pl.when(jnp.logical_not(self.nb.exists(side)))
            def _(side=side):
                rows = self.lay.region(side)
                self.near[rows, :] = jnp.zeros((rows.stop - rows.start, self.near.shape[1]), self.near.dtype)

    def arrive(self):
        for i, side in enumerate(SIDES):

            @pl.when(self.nb.exists(opposite(side)))
            def _(i=i):
                self.copy(i).wait_recv()

    def sent(self):
        for i, side in enumerate(SIDES):

            @pl.when(self.nb.exists(side))
            def _(i=i):
                self.copy(i).wait_send()


def edge_source(lay, flat, sides, corners):
    n = REACH * lay.n_f

    def source(side):
        dt, df = side
        if df == 0:
            return flat.at[pl.ds(0 if dt < 0 else lay.own - n, n)]
        if dt == 0:
            return sides.at[0 if df < 0 else 1]
        return corners.at[(dt + 1) + (df + 1) // 2]

    return source


def project_kernel(lay, *refs):
    tok, tok_s, tok_c, grad, wq, wk, wv, wo = refs[:8]
    q_ref, k_ref, v_ref, g_ref, hid_ref = refs[8:13]
    near_tok, hidden, wq_v, wk_v, wv_v, wo_v, w_sem, s_tok, r_tok = refs[13:]
    Neighbours().greet()
    toks = Exchange(lay, near_tok, edge_source(lay, tok, tok_s, tok_c), s_tok, r_tok)
    toks.start()
    loads = [
        pltpu.make_async_copy(src, dst, w_sem.at[i])
        for i, (src, dst) in enumerate(((wq, wq_v), (wk, wk_v), (wv, wv_v), (wo, wo_v)))
    ]
    for load in loads:
        load.start()
    toks.clear()

    def normalize(src, shift, start, stop):
        @pl.loop(0, (stop - start) // 32)
        def _(i):
            at = pl.multiple_of(start + i * 32, 32)
            wide = src[pl.ds(pl.multiple_of(at - shift, 32), 32), :].astype(F32)
            center = jnp.mean(wide, axis=-1, keepdims=True)
            shifted = wide - center
            inverse = lax.rsqrt(jnp.mean(shifted * shifted, axis=-1, keepdims=True) + EPS)
            hidden[pl.ds(at, 32), :] = (shifted * inverse).astype(BF16)

    a, b = lay.start, lay.start + lay.own
    normalize(tok, a, a, b)
    hid_ref[...] = hidden[a:b, :]
    for load in loads:
        load.wait()

    def rows(start, stop):
        for dst, w in ((q_ref, wq_v), (k_ref, wk_v), (v_ref, wv_v)):
            dst[start:stop, :] = nn(hidden[start:stop, :], w[...]).astype(BF16)

    rows(a, b)
    g_ref[...] = nt(grad[...], wo_v[...]).astype(BF16)
    toks.arrive()
    for start, stop in ((0, a), (b, lay.all)):
        normalize(near_tok, 0, start, stop)
        rows(start, stop)
    toks.sent()


def strips(lay, m):
    n_t, n_f, model = m.shape
    sides = jnp.stack([m[:, :REACH], m[:, n_f - REACH :]]).reshape(2, REACH * n_t, model)
    corners = jnp.stack(
        [m[t, f].reshape(REACH * REACH, model) for t in (slice(0, REACH), slice(n_t - REACH, n_t))
         for f in (slice(0, REACH), slice(n_f - REACH, n_f))]
    )
    return sides, jnp.pad(corners, ((0, 0), (0, lay.corner - REACH * REACH), (0, 0)))


def project(lay, tokens, d_out, weights):
    model = tokens.shape[-1]
    vm, any_ = pl.BlockSpec(memory_space=pltpu.VMEM), pl.BlockSpec(memory_space=pl.ANY)
    ext = jax.ShapeDtypeStruct((lay.all, model), BF16)
    sem = pltpu.SemaphoreType.DMA((len(SIDES),))
    return pl.pallas_call(
        functools.partial(project_kernel, lay),
        out_shape=[ext] * 3 + [jax.ShapeDtypeStruct((lay.own, model), BF16)] * 2,
        in_specs=[vm] * 4 + [any_] * 4,
        out_specs=[vm] * 5,
        scratch_shapes=[pltpu.VMEM((lay.all, model), BF16)] * 2
        + [pltpu.VMEM(w.shape, BF16) for w in weights]
        + [pltpu.SemaphoreType.DMA((4,))]
        + [sem] * 2,
        compiler_params=pltpu.CompilerParams(
            collective_id=2, has_side_effects=True, vmem_limit_bytes=48 * 1024 * 1024
        ),
    )(
        tokens.reshape(lay.own, model),
        *strips(lay, tokens),
        d_out.reshape(lay.own, model),
        *weights,
    )


def stats_kernel(lay, stat, att, tok, wo, own_g, far, near_ref, out_ref, g_ref, near, sides, corners, s_sem, r_sem):
    n_t, n_f = lay.n_t, lay.n_f
    Neighbours().greet()
    corners[...] = jnp.zeros(corners.shape, F32)
    for t in range(n_t):
        sides[0, t * REACH : (t + 1) * REACH, :] = stat[t * n_f : t * n_f + REACH, :]
        sides[1, t * REACH : (t + 1) * REACH, :] = stat[(t + 1) * n_f - REACH : (t + 1) * n_f, :]
    for j, first in enumerate((0, n_t - REACH)):
        for r in range(REACH):
            at = (first + r) * n_f
            corners[2 * j, r * REACH : (r + 1) * REACH, :] = stat[at : at + REACH, :]
            corners[2 * j + 1, r * REACH : (r + 1) * REACH, :] = stat[at + n_f - REACH : at + n_f, :]
    ex = Exchange(lay, near, edge_source(lay, stat, sides, corners), s_sem, r_sem)
    ex.start()
    ex.clear()
    near[lay.region((0, 0)), :] = stat[...]
    out_ref[...] = (tok[...].astype(F32) + nn(att[...], wo[...])).astype(BF16)
    a, b = lay.start, lay.start + lay.own
    g_ref[:a, :] = nt(far[:a, :], wo[...]).astype(BF16)
    g_ref[a:b, :] = own_g[...]
    g_ref[b:, :] = nt(far[b:, :], wo[...]).astype(BF16)
    ex.arrive()
    for half in range(2):
        near_ref[half] = near[lay.reach(half), :].T
    ex.sent()


def exchange_stats(lay, stats, attended, flat, w_out, grad_att, far):
    vm = pl.BlockSpec(memory_space=pltpu.VMEM)
    sem = pltpu.SemaphoreType.DMA((len(SIDES),))
    return pl.pallas_call(
        functools.partial(stats_kernel, lay),
        out_shape=[
            jax.ShapeDtypeStruct((2, 128, lay.span), F32),
            jax.ShapeDtypeStruct(flat.shape, BF16),
            jax.ShapeDtypeStruct(far.shape, BF16),
        ],
        in_specs=[vm] * 6,
        out_specs=[vm] * 3,
        scratch_shapes=[
            pltpu.VMEM((lay.all, 128), F32),
            pltpu.VMEM((2, REACH * lay.n_t, 128), F32),
            pltpu.VMEM((4, lay.corner, 128), F32),
            sem,
            sem,
        ],
        compiler_params=pltpu.CompilerParams(
            collective_id=3, has_side_effects=True, vmem_limit_bytes=24 * 1024 * 1024
        ),
    )(stats, attended, flat, w_out, grad_att, far)


def log2(n):
    return n.bit_length() - 1


def axis_orders(t_size, f_size):
    rest = [("freq", b) for b in range(log2(f_size))] + [("tm", b) for b in range(1, log2(t_size))]
    head, last = rest[:-1], rest[-1:]
    turns = [head[i:] + head[:i] for i in (2, 1, 0)] + [[head[1], head[0]] + head[2:]]
    return [[("tm", 0)] + turn + last for turn in turns]


def scatter_kernel(orders, sizes, *refs):
    n_mat = len(orders)
    n_st = len(orders[0])
    lefts = refs[:n_mat]
    rights = refs[n_mat : 2 * n_mat]
    out_ref = refs[2 * n_mat]
    total = refs[2 * n_mat + 1]
    sends = refs[2 * n_mat + 2 : 2 * n_mat + 2 + n_st]
    lands = refs[2 * n_mat + 2 + n_st : 2 * n_mat + 2 + 2 * n_st]
    send_sem, recv_sem = refs[-2:]
    tm, fq = lax.axis_index("tm"), lax.axis_index("freq")

    def bit(dim):
        axis, b = dim
        return ((tm if axis == "tm" else fq) // (1 << b)) % 2

    def partner(dim):
        axis, b = dim
        move = (1 - 2 * bit(dim)) * (1 << b)
        return (tm + move, fq) if axis == "tm" else (tm, fq + move)

    barrier = pltpu.get_barrier_semaphore()
    for dim in orders[0]:
        pl.semaphore_signal(barrier, inc=1, device_id=partner(dim), device_id_type=MESH)
    pl.semaphore_wait(barrier, n_st)

    def copy(m, st):
        return pltpu.make_async_remote_copy(
            src_ref=sends[st].at[m],
            dst_ref=lands[st].at[m],
            send_sem=send_sem.at[m, st],
            recv_sem=recv_sem.at[m, st],
            device_id=partner(orders[m][st]),
            device_id_type=MESH,
        )

    turn = list(range(n_mat - 1, -1, -1))
    half = sizes[0]
    for m in turn:
        theirs = pl.multiple_of((1 - bit(orders[m][0])) * half, half)
        sends[0][m] = nn(lefts[m][pl.ds(theirs, half), :], rights[m][...]).astype(BF16)
        copy(m, 0).start()
    for m in turn:
        mine = pl.multiple_of(bit(orders[m][0]) * half, half)
        total[m] = nn(lefts[m][pl.ds(mine, half), :], rights[m][...])
    base = [0] * n_mat
    for st in range(1, n_st):
        half = sizes[st]
        for m in turn:
            copy(m, st - 1).wait()
            b = bit(orders[m][st])
            theirs, mine = (1 - b) * half, b * half
            if half >= 16:
                theirs, mine = pl.multiple_of(theirs, half), pl.multiple_of(mine, half)
                there = pl.multiple_of(base[m] + theirs, half)
                here = pl.multiple_of(base[m] + mine, half)
                away = total[m, pl.ds(there, half), :] + lands[st - 1][m, pl.ds(theirs, half), :].astype(F32)
                sends[st][m] = away.astype(BF16)
                copy(m, st).start()
                total[m, pl.ds(here, half), :] += lands[st - 1][m, pl.ds(mine, half), :].astype(F32)
            else:
                start = pl.multiple_of(base[m], 2 * half)
                both = total[m, pl.ds(start, 2 * half), :] + lands[st - 1][m].astype(F32)
                low, high = both[:half], both[half:]
                away = jnp.where(b == 0, high, low)
                sends[st][m] = jnp.concatenate([away, away], axis=0).astype(BF16)
                copy(m, st).start()
                here = pl.multiple_of(base[m] + mine, half)
                total[m, pl.ds(here, half), :] = jnp.where(b == 0, low, high)
            base[m] = here
    half = sizes[-1]
    for m in turn:
        copy(m, n_st - 1).wait()
        out_ref[m] = total[m, pl.ds(base[m], half), :] + lands[-1][m].astype(F32)[0:half]


def scatter_sum(lefts, rights, t_size, f_size):
    n_dev = t_size * f_size
    n_st = log2(n_dev)
    orders = axis_orders(t_size, f_size)
    tokens, model = lefts[0].shape
    rows = model // n_dev
    sizes = [model >> (s + 1) for s in range(n_st)]
    flipped = []
    for left, order in zip(lefts, orders):
        place = [
            log2(t_size) - 1 - b if axis == "tm" else log2(t_size) + log2(f_size) - 1 - b for axis, b in order
        ]
        cube = left.T.reshape((2,) * n_st + (rows, tokens))
        flipped.append(cube.transpose(place + [n_st, n_st + 1]).reshape(model, tokens))
    n_mat = len(orders)
    blocks = [(n_mat, max(s, 16), model) for s in sizes]
    vm = pl.BlockSpec(memory_space=pltpu.VMEM)
    return pl.pallas_call(
        functools.partial(scatter_kernel, orders, sizes),
        out_shape=jax.ShapeDtypeStruct((n_mat, rows, model), F32),
        in_specs=[vm] * (2 * n_mat),
        out_specs=vm,
        scratch_shapes=[pltpu.VMEM((n_mat, sizes[0], model), F32)]
        + [pltpu.VMEM(b, BF16) for b in blocks]
        + [pltpu.VMEM(b, BF16) for b in blocks]
        + [pltpu.SemaphoreType.DMA((n_mat, n_st)), pltpu.SemaphoreType.DMA((n_mat, n_st))],
        compiler_params=pltpu.CompilerParams(
            collective_id=1, has_side_effects=True, vmem_limit_bytes=56 * 1024 * 1024
        ),
        cost_estimate=pl.CostEstimate(
            flops=2 * n_mat * tokens * model * model, bytes_accessed=4 * tokens * model, transcendentals=0
        ),
    )(*flipped, *rights)


def layer_norm(flat_rows):
    wide = flat_rows.astype(F32)
    center = jnp.mean(wide, axis=-1, keepdims=True)
    shifted = wide - center
    inverse = lax.rsqrt(jnp.mean(shifted * shifted, axis=-1, keepdims=True) + EPS)
    return shifted * inverse, inverse


def local(tokens, w_query, w_key, w_value, w_out, d_out):
    n_t, n_f, model = tokens.shape
    lay = Layout(n_t, n_f)
    flat = tokens.reshape(lay.own, model)
    grad_flat = d_out.reshape(lay.own, model)
    normed, inverse = layer_norm(flat)
    bias = window_bias(lay)
    query, key, value, grad_att, hidden = project(lay, tokens, d_out, (w_query, w_key, w_value, w_out))
    first, second = attention_calls(lay, model // HEADS, model)
    attended, grad_query, stats, far = first(query, grad_att, key, value, bias, grad_flat, *strips(lay, d_out))
    near_stats, output, near_gatt = exchange_stats(lay, stats, attended, flat, w_out, grad_att, far)
    grad_key, grad_value = second(key, value, query, near_gatt, bias, near_stats)

    weight_grads = scatter_sum(
        [hidden, hidden, hidden, attended],
        [grad_query, grad_key, grad_value, grad_flat],
        lax.axis_size("tm"),
        lax.axis_size("freq"),
    ).transpose(1, 0, 2)

    grad_hidden = nt(grad_query, w_query) + nt(grad_key, w_key) + nt(grad_value, w_value)
    center = jnp.mean(grad_hidden, axis=-1, keepdims=True)
    along = jnp.mean(grad_hidden * normed, axis=-1, keepdims=True)
    input_grad = (grad_flat.astype(F32) + (grad_hidden - center - normed * along) * inverse).astype(BF16)
    return output.reshape(n_t, n_f, model), input_grad.reshape(n_t, n_f, model), weight_grads


def solution(mesh):
    tile = P("tm", "freq", None)
    in_specs = (tile, P(), P(), P(), P(), tile)
    out_specs = (tile, tile, P(("tm", "freq"), None, None))
    return jax.shard_map(local, mesh=mesh, in_specs=in_specs, out_specs=out_specs, check_vma=False)
```

profile of v0, /device:TPU:0, one launch (start us, length us, event | category | flops | bytes accessed | tf_op | source)
XLA Modules:
  0.0 168.1 jit_solution(11715979923824716708)
XLA Ops:
  0.6 1.1 fusion.282
  2.9 30.0 %shard_map.85 = (bf16[832,1024]{1,0:T(8,128)(2,1)S(1)}, bf16[832,1024]{1,0:T(8,128)(2,1)}, bf16[832,1024]{1,0:T(8,128)(2,1)}, bf16[256,1024]{1,0:T(8,128)(2,1)S(1)}, bf16[256,1024]{1,0:T(8,128)(2,1)S(1)}) custom-call(bf16[256,1024]{1,0:T(8,128)(2,1)S(1)} %bitcast.30, bf16[2,96,1024]{2,1,0:T(8,128)(2,1)S(1)} %pad_maximum_fusion.1.refs_1_, ...), custom_call_target="tpu_custom_call" | custom-call | tf_op jit(solution)/shard_map/pallas_call | solution.py:348
  35.9 1.6 stack_reshape.28
  37.5 1.6 stack_reshape.29
  39.0 1.6 stack_reshape.30
  41.2 1.8 %fusion.15.refs_7_ = bf16[4,48,1024]{2,1,0:T(8,128)(2,1)} fusion(bf16[1,36,1024]{2,1,0:T(8,128)(2,1)} %stack_reshape.31, bf16[1,36,1024]{2,1,0:T(8,128)(2,1)} %stack_reshape.30, bf16[1,36,1024]{2,1,0:T(8,128)(2,1)} %stack_reshape.29, bf16[1,36,1024]{2,1,0:T(8,128)(2,1)} %stack_reshape.28), kind=kLoop, calls=%fused_computation.24 | loop fusion | flops 2555904 | bytes 688128 | tf_op jit(solution)/shard_map/stack | solution.py:336
  43.0 0.9 fusion.281
  43.9 1.7 %stack.34 = bf16[1,96,1024]{2,1,0:T(8,128)(2,1)} reshape(bf16[16,6,1024]{2,1,0:T(8,128)(2,1)} %get-tuple-element.43) | data formatting | bytes 393216 | tf_op jit(solution)/shard_map/stack | solution.py:335
  45.6 1.7 %stack.35 = bf16[1,96,1024]{2,1,0:T(8,128)(2,1)} reshape(bf16[16,6,1024]{2,1,0:T(8,128)(2,1)} %get-tuple-element.44) | data formatting | bytes 393216 | tf_op jit(solution)/shard_map/stack | solution.py:335
  47.3 1.1 pad_maximum_fusion.2.refs_6_
  48.4 1.4 copy-done.4
  49.8 1.5 copy-done.5
  51.3 1.0 copy-done.9
  52.3 1.0 copy-done.10
  53.3 19.1 %shard_map.86 = (bf16[256,1024]{1,0:T(8,128)(2,1)S(1)}, bf16[256,1024]{1,0:T(8,128)(2,1)S(1)}, f32[256,128]{1,0:T(8,128)S(1)}, bf16[832,1024]{1,0:T(8,128)(2,1)S(1)}) custom-call(bf16[832,1024]{1,0:T(8,128)(2,1)S(1)} %get-tuple-element.17.refs_0_.q_ref, bf16[256,1024]{1,0:T(8,128)(2,1)S(1)} %copy-done.9, bf16[832,1024]{1,0:T(8,128)(2,1)S(1)} %copy-done.4, ...), custom_call_target="tpu_custom_call" | custom-call | tf_op jit(solution)/shard_map/pallas_call | solution.py:559
  72.4 11.7 %shard_map.87 = (f32[2,128,640]{2,1,0:T(8,128)S(1)}, bf16[256,1024]{1,0:T(8,128)(2,1)S(1)}, bf16[832,1024]{1,0:T(8,128)(2,1)S(1)}) custom-call(f32[256,128]{1,0:T(8,128)S(1)} %get-tuple-element.21.stat, bf16[256,1024]{1,0:T(8,128)(2,1)S(1)} %get-tuple-element.22.att, bf16[256,1024]{1,0:T(8,128)(2,1)S(1)} %bitcast.31, bf16[1024,1024]{1,0:T(8,128)(2,1)S(1)} %copy-done.3, ...), custom_call_target="tpu_custom_call" | custom-call | tf_op jit(solution)/shard_map/pallas_call | solution.py:398
  85.0 9.7 %shard_map.88 = (bf16[256,1024]{1,0:T(8,128)(2,1)S(1)}, bf16[256,1024]{1,0:T(8,128)(2,1)S(1)}) custom-call(bf16[832,1024]{1,0:T(8,128)(2,1)S(1)} %copy-done.4, bf16[832,1024]{1,0:T(8,128)(2,1)S(1)} %copy-done.5, bf16[832,1024]{1,0:T(8,128)(2,1)S(1)} %get-tuple-element.17.refs_0_.q_ref, bf16[832,1024]{1,0:T(8,128)(2,1)S(1)} %get-tuple-element.26.g_ref, ...), custom_call_target="tpu_custom_call" | custom-call | tf_op jit(solution)/shard_map/pallas_call | solution.py:561
  96.5 0.8 copy.19
  97.6 0.9 copy.17
  100.1 57.3 %shard_map.89 = f32[4,32,1024]{2,1,0:T(8,128)} custom-call(bf16[1024,256]{1,0:T(8,128)(2,1)} %bitcast.45, bf16[1024,256]{1,0:T(8,128)(2,1)} %bitcast.46, bf16[1024,256]{1,0:T(8,128)(2,1)} %bitcast.44, bf16[1024,256]{1,0:T(8,128)(2,1)} %bitcast.43, bf16[256,1024]{1,0:T(8,128)(2,1)} %copy-done.13, bf16[256,1024]{1,0:T(8,128)(2,1)} %copy-done.15, ...), custom_call_target="tpu_custom_call" | custom-call | flops 2147483648 | bytes 1048576 | tf_op jit(solution)/shard_map/pallas_call | solution.py:524
  157.4 2.2 %copy.20 = f32[32,4,1024]{2,1,0:T(4,128)} copy(f32[32,4,1024]{2,0,1:T(8,128)} %bitcast.47) | data formatting | bytes 1048576
  161.3 1.8 %convolution_add_fusion.1 = f32[256,1024]{1,0:T(8,128)} fusion(f32[256,1024]{1,0:T(8,128)S(1)} %fusion.284, bf16[256,1024]{1,0:T(8,128)(2,1)S(1)} %copy-done.16, bf16[1024,1024]{1,0:T(8,128)(2,1)S(1)} %copy-done.22), kind=kOutput, calls=%fused_computation.1 | convolution fusion | flops 537133056 | bytes 4718592 | tf_op jit(solution)/shard_map/dot_general | solution.py:25
  163.8 2.2 %fusion.279 = (f32[256]{0:T(256)S(1)}, f32[256]{0:T(256)S(1)}, f32[256,1024]{1,0:T(8,128)S(1)}) fusion(f32[256]{0:T(256)S(1)} %rsqrt.12, f32[256]{0:T(256)S(1)} %div.301, bf16[16,16,1024]{2,1,0:T(8,128)(2,1)S(1)} %copy-done, f32[256,1024]{1,0:T(8,128)} %convolution_add_fusion.1, bf16[256,1024]{1,0:T(8,128)(2,1)S(1)} %copy-done.12, ...), kind=kOutput, calls=%fused_computation.364 | convolution fusion | flops 538705408 | bytes 5246976 | tf_op jit(solution)/shard_map/dot_general | solution.py:25
  166.1 1.2 add_convert_fusion
  (77 shorter events, 12.3 us)
Async XLA Ops:
  0.6 1.4 copy-start
  1.8 1.1 copy-start.1
  32.9 0.8 copy-start.8
  33.7 0.8 copy-start.17
  48.3 1.5 copy-start.4
  49.8 1.5 copy-start.5
  51.3 1.0 copy-start.9
  52.3 1.0 copy-start.10
  53.3 19.1 %copy-start.3 = (bf16[1024,1024]{1,0:T(8,128)(2,1)S(1)}, bf16[1024,1024]{1,0:T(8,128)(2,1)}, u32[]{:S(2)}) copy-start(bf16[1024,1024]{1,0:T(8,128)(2,1)} %wo.1) | copy-start | bytes 6291460
  72.4 11.8 %copy-start.6 = (bf16[256,1024]{1,0:T(8,128)(2,1)}, bf16[256,1024]{1,0:T(8,128)(2,1)S(1)}, u32[]{:S(2)}) copy-start(bf16[256,1024]{1,0:T(8,128)(2,1)S(1)} %get-tuple-element.22.att) | copy-start | bytes 1572868
  72.4 11.8 %copy-start.13 = (bf16[256,1024]{1,0:T(8,128)(2,1)}, bf16[256,1024]{1,0:T(8,128)(2,1)S(1)}, u32[]{:S(2)}) copy-start(bf16[256,1024]{1,0:T(8,128)(2,1)S(1)} %get-tuple-element.25.refs_4_) | copy-start | bytes 1572868
  84.2 0.8 copy-start.19
  85.0 11.3 %copy-start.7 = (bf16[256,1024]{1,0:T(8,128)(2,1)S(1)}, bf16[256,1024]{1,0:T(8,128)(2,1)}, u32[]{:S(2)}) copy-start(bf16[256,1024]{1,0:T(8,128)(2,1)} %copy-done.6) | copy-start | bytes 1572868
  94.7 0.8 copy-start.11
  95.5 0.8 copy-start.15
  96.3 1.1 copy-start.18
  100.1 59.5 %copy-start.14 = (bf16[256,1024]{1,0:T(8,128)(2,1)S(1)}, bf16[256,1024]{1,0:T(8,128)(2,1)}, u32[]{:S(2)}) copy-start(bf16[256,1024]{1,0:T(8,128)(2,1)} %copy-done.13) | copy-start | bytes 1572868
  100.1 59.5 %copy-start.21 = (bf16[1024,1024]{1,0:T(8,128)(2,1)S(1)}, bf16[1024,1024]{1,0:T(8,128)(2,1)}, u32[]{:S(2)}) copy-start(bf16[1024,1024]{1,0:T(8,128)(2,1)} %refs_4_.1) | copy-start | bytes 6291460
  159.6 1.0 copy-start.16
  159.6 1.8 %copy-start.22 = (bf16[1024,1024]{1,0:T(8,128)(2,1)S(1)}, bf16[1024,1024]{1,0:T(8,128)(2,1)}, u32[]{:S(2)}) copy-start(bf16[1024,1024]{1,0:T(8,128)(2,1)} %refs_5_.1) | copy-start | bytes 6291460
  161.3 2.5 %copy-start.12 = (bf16[256,1024]{1,0:T(8,128)(2,1)S(1)}, bf16[256,1024]{1,0:T(8,128)(2,1)}, u32[]{:S(2)}) copy-start(bf16[256,1024]{1,0:T(8,128)(2,1)} %copy-done.11) | copy-start | bytes 1572868
  161.3 2.5 %copy-start.23 = (bf16[1024,1024]{1,0:T(8,128)(2,1)S(1)}, bf16[1024,1024]{1,0:T(8,128)(2,1)}, u32[]{:S(2)}) copy-start(bf16[1024,1024]{1,0:T(8,128)(2,1)} %refs_6_.1) | copy-start | bytes 6291460
  163.8 2.3 %copy-start.2 = (bf16[16,16,1024]{2,1,0:T(8,128)(2,1)S(1)}, bf16[16,16,1024]{2,1,0:T(8,128)(2,1)}, u32[]{:S(2)}) copy-start(bf16[16,16,1024]{2,1,0:T(8,128)(2,1)} %param.11) | copy-start | bytes 1572868
  166.1 1.3 copy-start.20
where the time goes:
time: 169 us; the launch traced here: 168 us
  Pallas kernels  128 us (76%)
  local copies, waits for them, and re-layouts  29.2 us (17%)
  other arithmetic  5.25 us (3%)
  matrix products  4.81 us (3%)
    pallas_call x1, Pallas kernels, scatter_sum(): pl.pallas_call(functools.partial(scatter_kernel, orders, sizes), out_shap...  57.3 us
    pallas_call x1, Pallas kernels, project(): pl.pallas_call(functools.partial(project_kernel, lay), out_shape=[ext] *...  30 us
    pallas_call x1, Pallas kernels, local(): first(query, grad_att, key, value, bias, grad_flat, *strips(lay, d_out))  19.1 us
    unnamed x50, local copies, waits for them, and re-layouts  13.5 us
    pallas_call x1, Pallas kernels, exchange_stats(): pl.pallas_call(functools.partial(stats_kernel, lay), out_shape=[jax.Shape...  11.7 us
    pallas_call x1, Pallas kernels, local(): second(key, value, query, near_gatt, bias, near_stats)  9.7 us
    another operation x8, local copies, waits for them, and re-layouts, strips(): jnp.stack([m[t, f].reshape(REACH * REACH, model) for t in (slice(0, REACH...  5.44 us
    dot_general x3, matrix products, nt(): lax.dot_general(a, b, (((1,), (1,)), ((), ())), preferred_element_type=F32)  4.81 us

commit v1 on v0

--- a/solution.py
+++ b/solution.py
@@ -68,21 +68,24 @@
         ex.sent()
 
 
-def key_kernel(scale, lay, k_ref, v_ref, q_ref, g_ref, bias_ref, stat_ref, gk_ref, gv_ref):
-    h = pl.program_id(0)
+def key_pass(scale, lay, width, k_ref, v_ref, q_ref, g_ref, bias_ref, stat_ref, gk_ref, gv_ref):
     n_q = lay.own // 2
-    for half in range(2):
-        out = slice(half * n_q, (half + 1) * n_q)
-        rows = slice(lay.start + half * n_q, lay.start + (half + 1) * n_q)
-        cols = lay.reach(half)
-        q = q_ref[cols, :]
-        g = g_ref[cols, :]
-        s = nt(k_ref[rows, :], q) * scale + bias_ref[half]
-        probs = jnp.exp(s - stat_ref[half, pl.ds(2 * h, 1), :])
-        gv_ref[out, :] = nn(probs.astype(BF16), g).astype(BF16)
-        gp = nt(v_ref[rows, :], g)
-        gs = (probs * (gp - stat_ref[half, pl.ds(2 * h + 1, 1), :]) * scale).astype(BF16)
-        gk_ref[out, :] = nn(gs, q).astype(BF16)
+
+    @pl.loop(0, HEADS)
+    def _(h):
+        lanes = pl.ds(pl.multiple_of(h * width, width), width)
+        for half in range(2):
+            out = slice(half * n_q, (half + 1) * n_q)
+            rows = slice(lay.start + half * n_q, lay.start + (half + 1) * n_q)
+            cols = lay.reach(half)
+            q = q_ref[cols, lanes]
+            g = g_ref[cols, lanes]
+            s = nt(k_ref[rows, lanes], q) * scale + bias_ref[half]
+            probs = jnp.exp(s - stat_ref[half, pl.ds(2 * h, 1), :])
+            gv_ref[out, lanes] = nn(probs.astype(BF16), g).astype(BF16)
+            gp = nt(v_ref[rows, lanes], g)
+            gs = (probs * (gp - stat_ref[half, pl.ds(2 * h + 1, 1), :]) * scale).astype(BF16)
+            gk_ref[out, lanes] = nn(gs, q).astype(BF16)
 
 
 def attention_calls(lay, width, model):
@@ -113,15 +116,7 @@
             collective_id=4, has_side_effects=True, vmem_limit_bytes=32 * 1024 * 1024
         ),
     )
-    second = pl.pallas_call(
-        functools.partial(key_kernel, scale, lay),
-        grid=(HEADS,),
-        in_specs=[ext, ext, ext, ext, bias, pl.BlockSpec((2, 128, lay.span), lambda h: (0, 0, 0))],
-        out_specs=[own, own],
-        out_shape=[big, big],
-        compiler_params=params,
-    )
-    return first, second
+    return first
 
 
 SIDES = ((0, 1), (0, -1), (1, 0), (-1, 0), (1, 1), (1, -1), (-1, 1), (-1, -1))
@@ -287,9 +282,9 @@
 
 
 def project_kernel(lay, *refs):
-    tok, tok_s, tok_c, grad, wq, wk, wv, wo = refs[:8]
-    q_ref, k_ref, v_ref, g_ref, hid_ref = refs[8:13]
-    near_tok, hidden, wq_v, wk_v, wv_v, wo_v, w_sem, s_tok, r_tok = refs[13:]
+    tok, tok_s, tok_c, grad, grad_s, grad_c, wq, wk, wv, wo = refs[:10]
+    q_ref, k_ref, v_ref, g_ref, hid_ref, side_ref, corner_ref = refs[10:17]
+    near_tok, hidden, wq_v, wk_v, wv_v, wo_v, w_sem, s_tok, r_tok = refs[17:]
     Neighbours().greet()
     toks = Exchange(lay, near_tok, edge_source(lay, tok, tok_s, tok_c), s_tok, r_tok)
     toks.start()
@@ -300,6 +295,8 @@
     for load in loads:
         load.start()
     toks.clear()
+    side_ref[...] = grad_s[...]
+    corner_ref[...] = grad_c[...]
 
     def normalize(src, shift, start, stop):
         @pl.loop(0, (stop - start) // 32)
@@ -344,12 +341,15 @@
     model = tokens.shape[-1]
     vm, any_ = pl.BlockSpec(memory_space=pltpu.VMEM), pl.BlockSpec(memory_space=pl.ANY)
     ext = jax.ShapeDtypeStruct((lay.all, model), BF16)
+    grad_strips = strips(lay, d_out)
     sem = pltpu.SemaphoreType.DMA((len(SIDES),))
     return pl.pallas_call(
         functools.partial(project_kernel, lay),
-        out_shape=[ext] * 3 + [jax.ShapeDtypeStruct((lay.own, model), BF16)] * 2,
-        in_specs=[vm] * 4 + [any_] * 4,
-        out_specs=[vm] * 5,
+        out_shape=[ext] * 3
+        + [jax.ShapeDtypeStruct((lay.own, model), BF16)] * 2
+        + [jax.ShapeDtypeStruct(a.shape, BF16) for a in grad_strips],
+        in_specs=[vm] * 6 + [any_] * 4,
+        out_specs=[vm] * 7,
         scratch_shapes=[pltpu.VMEM((lay.all, model), BF16)] * 2
         + [pltpu.VMEM(w.shape, BF16) for w in weights]
         + [pltpu.SemaphoreType.DMA((4,))]
@@ -361,6 +361,7 @@
         tokens.reshape(lay.own, model),
         *strips(lay, tokens),
         d_out.reshape(lay.own, model),
+        *grad_strips,
         *weights,
     )
 
@@ -428,15 +429,16 @@
     return [[("tm", 0)] + turn + last for turn in turns]
 
 
-def scatter_kernel(orders, sizes, *refs):
+def scatter_kernel(orders, sizes, scale, lay, width, *refs):
     n_mat = len(orders)
     n_st = len(orders[0])
     lefts = refs[:n_mat]
-    rights = refs[n_mat : 2 * n_mat]
-    out_ref = refs[2 * n_mat]
-    total = refs[2 * n_mat + 1]
-    sends = refs[2 * n_mat + 2 : 2 * n_mat + 2 + n_st]
-    lands = refs[2 * n_mat + 2 + n_st : 2 * n_mat + 2 + 2 * n_st]
+    gq_ref, do_ref = refs[n_mat : n_mat + 2]
+    key_ins = refs[n_mat + 2 : n_mat + 8]
+    out_ref, gk_ref, gv_ref, total = refs[n_mat + 8 : n_mat + 12]
+    rights = (gq_ref, gk_ref, gv_ref, do_ref)
+    sends = refs[n_mat + 12 : n_mat + 12 + n_st]
+    lands = refs[n_mat + 12 + n_st : n_mat + 12 + 2 * n_st]
     send_sem, recv_sem = refs[-2:]
     tm, fq = lax.axis_index("tm"), lax.axis_index("freq")
 
@@ -464,47 +466,73 @@
             device_id_type=MESH,
         )
 
-    turn = list(range(n_mat - 1, -1, -1))
-    half = sizes[0]
-    for m in turn:
+    base = [0] * n_mat
+
+    def begin(m):
+        half = sizes[0]
         theirs = pl.multiple_of((1 - bit(orders[m][0])) * half, half)
         sends[0][m] = nn(lefts[m][pl.ds(theirs, half), :], rights[m][...]).astype(BF16)
         copy(m, 0).start()
-    for m in turn:
+
+    def own_part(m):
+        half = sizes[0]
         mine = pl.multiple_of(bit(orders[m][0]) * half, half)
         total[m] = nn(lefts[m][pl.ds(mine, half), :], rights[m][...])
-    base = [0] * n_mat
-    for st in range(1, n_st):
+
+    def advance(m, st):
         half = sizes[st]
-        for m in turn:
-            copy(m, st - 1).wait()
-            b = bit(orders[m][st])
-            theirs, mine = (1 - b) * half, b * half
-            if half >= 16:
-                theirs, mine = pl.multiple_of(theirs, half), pl.multiple_of(mine, half)
-                there = pl.multiple_of(base[m] + theirs, half)
-                here = pl.multiple_of(base[m] + mine, half)
-                away = total[m, pl.ds(there, half), :] + lands[st - 1][m, pl.ds(theirs, half), :].astype(F32)
-                sends[st][m] = away.astype(BF16)
-                copy(m, st).start()
-                total[m, pl.ds(here, half), :] += lands[st - 1][m, pl.ds(mine, half), :].astype(F32)
-            else:
-                start = pl.multiple_of(base[m], 2 * half)
-                both = total[m, pl.ds(start, 2 * half), :] + lands[st - 1][m].astype(F32)
-                low, high = both[:half], both[half:]
-                away = jnp.where(b == 0, high, low)
-                sends[st][m] = jnp.concatenate([away, away], axis=0).astype(BF16)
-                copy(m, st).start()
-                here = pl.multiple_of(base[m] + mine, half)
-                total[m, pl.ds(here, half), :] = jnp.where(b == 0, low, high)
-            base[m] = here
+        copy(m, st - 1).wait()
+        b = bit(orders[m][st])
+        theirs, mine = (1 - b) * half, b * half
+        if half >= 16:
+            theirs, mine = pl.multiple_of(theirs, half), pl.multiple_of(mine, half)
+            there = pl.multiple_of(base[m] + theirs, half)
+            here = pl.multiple_of(base[m] + mine, half)
+            away = total[m, pl.ds(there, half), :] + lands[st - 1][m, pl.ds(theirs, half), :].astype(F32)
+            sends[st][m] = away.astype(BF16)
+            copy(m, st).start()
+            total[m, pl.ds(here, half), :] += lands[st - 1][m, pl.ds(mine, half), :].astype(F32)
+        else:
+            start = pl.multiple_of(base[m], 2 * half)
+            both = total[m, pl.ds(start, 2 * half), :] + lands[st - 1][m].astype(F32)
+            low, high = both[:half], both[half:]
+            away = jnp.where(b == 0, high, low)
+            sends[st][m] = jnp.concatenate([away, away], axis=0).astype(BF16)
+            copy(m, st).start()
+            here = pl.multiple_of(base[m] + mine, half)
+            total[m, pl.ds(here, half), :] = jnp.where(b == 0, low, high)
+        base[m] = here
+
+    early, late = (n_mat - 1, 0), (1, 2)
+    turn = early + late
+    for m in early:
+        begin(m)
+    for m in early:
+        own_part(m)
+    for m in early:
+        advance(m, 1)
+    key_pass(scale, lay, width, *key_ins, gk_ref, gv_ref)
+    for m in late:
+        begin(m)
+    for m in early:
+        advance(m, 2)
+    for m in late:
+        own_part(m)
+    for m in late:
+        advance(m, 1)
+    for st in range(2, n_st):
+        for m in early:
+            if st + 1 < n_st:
+                advance(m, st + 1)
+        for m in late:
+            advance(m, st)
     half = sizes[-1]
     for m in turn:
         copy(m, n_st - 1).wait()
         out_ref[m] = total[m, pl.ds(base[m], half), :] + lands[-1][m].astype(F32)[0:half]
 
 
-def scatter_sum(lefts, rights, t_size, f_size):
+def scatter_sum(lefts, grad_query, d_out, key_ins, lay, width, t_size, f_size):
     n_dev = t_size * f_size
     n_st = log2(n_dev)
     orders = axis_orders(t_size, f_size)
@@ -522,10 +550,11 @@
     blocks = [(n_mat, max(s, 16), model) for s in sizes]
     vm = pl.BlockSpec(memory_space=pltpu.VMEM)
     return pl.pallas_call(
-        functools.partial(scatter_kernel, orders, sizes),
-        out_shape=jax.ShapeDtypeStruct((n_mat, rows, model), F32),
-        in_specs=[vm] * (2 * n_mat),
-        out_specs=vm,
+        functools.partial(scatter_kernel, orders, sizes, 1.0 / math.sqrt(width), lay, width),
+        out_shape=[jax.ShapeDtypeStruct((n_mat, rows, model), F32)]
+        + [jax.ShapeDtypeStruct((tokens, model), BF16)] * 2,
+        in_specs=[vm] * (n_mat + 8),
+        out_specs=[vm] * 3,
         scratch_shapes=[pltpu.VMEM((n_mat, sizes[0], model), F32)]
         + [pltpu.VMEM(b, BF16) for b in blocks]
         + [pltpu.VMEM(b, BF16) for b in blocks]
@@ -536,7 +565,7 @@
         cost_estimate=pl.CostEstimate(
             flops=2 * n_mat * tokens * model * model, bytes_accessed=4 * tokens * model, transcendentals=0
         ),
-    )(*flipped, *rights)
+    )(*flipped, grad_query, d_out, *key_ins)
 
 
 def layer_norm(flat_rows):
@@ -554,18 +583,21 @@
     grad_flat = d_out.reshape(lay.own, model)
     normed, inverse = layer_norm(flat)
     bias = window_bias(lay)
-    query, key, value, grad_att, hidden = project(lay, tokens, d_out, (w_query, w_key, w_value, w_out))
-    first, second = attention_calls(lay, model // HEADS, model)
-    attended, grad_query, stats, far = first(query, grad_att, key, value, bias, grad_flat, *strips(lay, d_out))
+    query, key, value, grad_att, hidden, g_sides, g_corners = project(lay, tokens, d_out, (w_query, w_key, w_value, w_out))
+    first = attention_calls(lay, model // HEADS, model)
+    attended, grad_query, stats, far = first(query, grad_att, key, value, bias, grad_flat, g_sides, g_corners)
     near_stats, output, near_gatt = exchange_stats(lay, stats, attended, flat, w_out, grad_att, far)
-    grad_key, grad_value = second(key, value, query, near_gatt, bias, near_stats)
-
-    weight_grads = scatter_sum(
+    weight_grads, grad_key, grad_value = scatter_sum(
         [hidden, hidden, hidden, attended],
-        [grad_query, grad_key, grad_value, grad_flat],
+        grad_query,
+        grad_flat,
+        (key, value, query, near_gatt, bias, near_stats),
+        lay,
+        model // HEADS,
         lax.axis_size("tm"),
         lax.axis_size("freq"),
-    ).transpose(1, 0, 2)
+    )
+    weight_grads = weight_grads.transpose(1, 0, 2)
 
     grad_hidden = nt(grad_query, w_query) + nt(grad_key, w_key) + nt(grad_value, w_value)
     center = jnp.mean(grad_hidden, axis=-1, keepdims=True)

time: 169 us -> 156 us (0.923)
  local copies, waits for them, and re-layouts: 29.2 us -> 21.3 us
  other arithmetic: 5.25 us -> 2.48 us
  Pallas kernels: 128 us -> 126 us
    another operation x8, local copies, waits for them, and re-layouts: 5.44 us -> 0.24 us  [strips(): jnp.stack([m[t, f].reshape(REACH * REACH, model) for t in (slice(0, REACH...]
    another operation x4, local copies, waits for them, and re-layouts: 3.54 us -> 0.28 us  [strips(): jnp.stack([m[:, :REACH], m[:, n_f - REACH:]]).reshape(2, REACH * n_t, model)]
    pallas_call x3 -> x2, Pallas kernels: 86.1 us -> 84.2 us  [the longest x1 65.1 us: scatter_sum(): pl.pallas_call(functools.partial(scatter_kernel, orders, sizes, 1.0 / mat...]
    another operation x2 -> x1, other arithmetic: 1.82 us -> 0.08 us  [strips(): jnp.stack([m[t, f].reshape(REACH * REACH, model) for t in (slice(0, REACH...]
    unnamed x50 -> x52, local copies, waits for them, and re-layouts: 13.5 us -> 14.4 us
where the time goes in v1:
time: 156 us
  Pallas kernels  126 us (81%)
  local copies, waits for them, and re-layouts  21.3 us (14%)
  matrix products  4.85 us (3%)
  other arithmetic  2.48 us (2%)
    pallas_call x1, Pallas kernels, scatter_sum(): pl.pallas_call(functools.partial(scatter_kernel, orders, sizes, 1.0 / mat...  65.1 us
    pallas_call x1, Pallas kernels, project(): pl.pallas_call(functools.partial(project_kernel, lay), out_shape=[ext] *...  30.1 us
    pallas_call x1, Pallas kernels, local(): first(query, grad_att, key, value, bias, grad_flat, g_sides, g_corners)  19.1 us
    unnamed x52, local copies, waits for them, and re-layouts  14.4 us
    pallas_call x1, Pallas kernels, exchange_stats(): pl.pallas_call(functools.partial(stats_kernel, lay), out_shape=[jax.Shape...  11.7 us
    dot_general x3, matrix products, nt(): lax.dot_general(a, b, (((1,), (1,)), ((), ())), preferred_element_type=F32)  4.85 us
    transpose x4, local copies, waits for them, and re-layouts, scatter_sum(): cube.transpose(place + [n_st, n_st + 1]).reshape(model, tokens)  3.36 us

profile of v1, /device:TPU:0, one launch (start us, length us, event | category | flops | bytes accessed | tf_op | source)
XLA Modules:
  0.0 155.7 jit_solution(2024586067947639715)
XLA Ops:
  0.6 1.1 fusion.282
  1.9 1.1 fusion.280
  4.4 30.1 %shard_map.85 = (bf16[832,1024]{1,0:T(8,128)(2,1)S(1)}, bf16[832,1024]{1,0:T(8,128)(2,1)}, bf16[832,1024]{1,0:T(8,128)(2,1)}, bf16[256,1024]{1,0:T(8,128)(2,1)S(...) custom-call(bf16[256,1024]{1,0:T(8,128)(2,1)S(1)} %bitcast.30, ...), custom_call_target="tpu_custom_call" | custom-call | tf_op jit(solution)/shard_map/pallas_call | solution.py:346
  35.3 0.8 copy-done.14
  38.3 1.4 copy-done.5
  39.7 1.5 copy-done.6
  41.1 1.0 copy-done.11
  42.2 1.0 copy-done.17
  43.2 1.0 copy-done.19
  44.2 19.1 %shard_map.86 = (bf16[256,1024]{1,0:T(8,128)(2,1)S(1)}, bf16[256,1024]{1,0:T(8,128)(2,1)S(1)}, f32[256,128]{1,0:T(8,128)S(1)}, bf16[832,1024]{1,0:T(8,128)(2,1)S(1)}) custom-call(bf16[832,1024]{1,0:T(8,128)(2,1)S(1)} %get-tuple-element.20.refs_0_.refs_8_, bf16[256,1024]{1,0:T(8,128)(2,1)S(1)} %copy-done.11, bf16[832,1024]{1,0:T(8,128)(2,1)S(1)} %copy-done.5, ...), custom_call_target="tpu_custom_call" | custom-call | tf_op jit(solution)/shard_map/pallas_call | solution.py:588
  63.3 11.7 %shard_map.87 = (f32[2,128,640]{2,1,0:T(8,128)S(1)}, bf16[256,1024]{1,0:T(8,128)(2,1)S(1)}, bf16[832,1024]{1,0:T(8,128)(2,1)S(1)}) custom-call(f32[256,128]{1,0:T(8,128)S(1)} %get-tuple-element.26.stat, bf16[256,1024]{1,0:T(8,128)(2,1)S(1)} %get-tuple-element.27.att, bf16[256,1024]{1,0:T(8,128)(2,1)S(1)} %bitcast.31, bf16[1024,1024]{1,0:T(8,128)(2,1)S(1)} %copy-done.3, ...), custom_call_target="tpu_custom_call" | custom-call | tf_op jit(solution)/shard_map/pallas_call | solution.py:399
  75.1 1.2 copy-done.12
  76.3 0.9 copy-done.13
  77.4 0.8 copy.19
  78.4 0.8 copy.17
  79.3 0.8 copy.15
  80.1 0.8 copy.16
  81.0 65.1 %shard_map.88 = (f32[4,32,1024]{2,1,0:T(8,128)}, bf16[256,1024]{1,0:T(8,128)(2,1)}, bf16[256,1024]{1,0:T(8,128)(2,1)}) custom-call(bf16[1024,256]{1,0:T(8,128)(2,1)} %bitcast.43, bf16[1024,256]{1,0:T(8,128)(2,1)} %bitcast.44, bf16[1024,256]{1,0:T(8,128)(2,1)} %bitcast.42, bf16[1024,256]{1,0:T(8,128)(2,1)} %bitcast.41, bf16[256,1024]{1,0:T(8,128)(2,1)} %copy-done.8, ...), custom_call_target="tpu_custom_call" | custom-call | flops 2147483648 | bytes 1048576 | tf_op jit(solution)/shard_map/pallas_call | solution.py:552
  146.9 0.8 copy-done.21
  147.7 1.7 %convolution_add_fusion.1 = f32[256,1024]{1,0:T(8,128)} fusion(f32[256,1024]{1,0:T(8,128)S(1)} %fusion.284, bf16[256,1024]{1,0:T(8,128)(2,1)S(1)} %copy-done.23, bf16[1024,1024]{1,0:T(8,128)(2,1)S(1)} %copy-done.21), kind=kOutput, calls=%fused_computation.1 | convolution fusion | flops 537133056 | bytes 4718592 | tf_op jit(solution)/shard_map/dot_general | solution.py:25
  150.1 2.4 %fusion.279 = (f32[256]{0:T(256)S(1)}, f32[256]{0:T(256)S(1)}, f32[256,1024]{1,0:T(8,128)S(1)}) fusion(f32[256]{0:T(256)S(1)} %rsqrt.12, f32[256]{0:T(256)S(1)} %div.301, bf16[16,16,1024]{2,1,0:T(8,128)(2,1)S(1)} %copy-done, f32[256,1024]{1,0:T(8,128)} %convolution_add_fusion.1, bf16[256,1024]{1,0:T(8,128)(2,1)} %get-tuple-element.35, ...), kind=kOutput, calls=%fused_computation.364 | convolution fusion | flops 538705408 | bytes 5246976 | tf_op jit(solution)/shard_map/dot_general | solution.py:25
  152.5 1.2 add_convert_fusion
  153.8 1.1 copy.20
  154.9 0.8 copy.22
  (76 shorter events, 6.2 us)
Async XLA Ops:
  0.6 2.7 %copy-start = (bf16[16,16,1024]{2,1,0:T(8,128)(2,1)S(1)}, bf16[16,16,1024]{2,1,0:T(8,128)(2,1)}, u32[]{:S(2)}) copy-start(bf16[16,16,1024]{2,1,0:T(8,128)(2,1)} %param.6) | copy-start | bytes 1572868
  3.0 1.0 copy-start.1
  34.5 0.8 copy-start.10
  35.3 0.8 copy-start.14
  36.9 0.8 copy-start.18
  37.6 25.7 %copy-start.4 = (bf16[832,1024]{1,0:T(8,128)(2,1)}, bf16[832,1024]{1,0:T(8,128)(2,1)S(1)}, u32[]{:S(2)}) copy-start(bf16[832,1024]{1,0:T(8,128)(2,1)S(1)} %get-tuple-element.20.refs_0_.refs_8_) | copy-start | bytes 5111812
  37.6 2.1 %copy-start.5 = (bf16[832,1024]{1,0:T(8,128)(2,1)S(1)}, bf16[832,1024]{1,0:T(8,128)(2,1)}, u32[]{:S(2)}) copy-start(bf16[832,1024]{1,0:T(8,128)(2,1)} %get-tuple-element.22.refs_2_.refs_6_) | copy-start | bytes 5111812
  39.7 1.5 copy-start.6
  41.1 1.0 copy-start.11
  42.2 1.0 copy-start.17
  43.2 1.0 copy-start.19
  44.2 19.1 %copy-start.7 = (f32[2,128,640]{2,1,0:T(8,128)}, f32[2,128,640]{2,1,0:T(8,128)S(1)}, u32[]{:S(2)}) copy-start(f32[2,128,640]{2,1,0:T(8,128)S(1)} %pad_maximum_fusion.refs_4_.refs_10_) | copy-start | bytes 1966084
  44.2 19.1 %copy-start.3 = (bf16[1024,1024]{1,0:T(8,128)(2,1)S(1)}, bf16[1024,1024]{1,0:T(8,128)(2,1)}, u32[]{:S(2)}) copy-start(bf16[1024,1024]{1,0:T(8,128)(2,1)} %wo.1) | copy-start | bytes 6291460
  63.3 11.8 %copy-start.8 = (bf16[256,1024]{1,0:T(8,128)(2,1)}, bf16[256,1024]{1,0:T(8,128)(2,1)S(1)}, u32[]{:S(2)}) copy-start(bf16[256,1024]{1,0:T(8,128)(2,1)S(1)} %get-tuple-element.30.refs_4_) | copy-start | bytes 1572868
  75.1 1.2 copy-start.12
  76.3 0.9 copy-start.13
  77.2 1.1 copy-start.15
  81.0 65.1 %copy-start.9 = (bf16[256,1024]{1,0:T(8,128)(2,1)S(1)}, bf16[256,1024]{1,0:T(8,128)(2,1)}, u32[]{:S(2)}) copy-start(bf16[256,1024]{1,0:T(8,128)(2,1)} %copy-done.8) | copy-start | bytes 1572868
  81.0 65.1 %copy-start.20 = (bf16[1024,1024]{1,0:T(8,128)(2,1)S(1)}, bf16[1024,1024]{1,0:T(8,128)(2,1)}, u32[]{:S(2)}) copy-start(bf16[1024,1024]{1,0:T(8,128)(2,1)} %refs_6_.1) | copy-start | bytes 6291460
  146.1 1.6 %copy-start.21 = (bf16[1024,1024]{1,0:T(8,128)(2,1)S(1)}, bf16[1024,1024]{1,0:T(8,128)(2,1)}, u32[]{:S(2)}) copy-start(bf16[1024,1024]{1,0:T(8,128)(2,1)} %refs_7_.1) | copy-start | bytes 6291460
  146.1 1.7 %copy-start.23 = (bf16[256,1024]{1,0:T(8,128)(2,1)S(1)}, bf16[256,1024]{1,0:T(8,128)(2,1)}, u32[]{:S(2)}) copy-start(bf16[256,1024]{1,0:T(8,128)(2,1)} %get-tuple-element.34) | copy-start | bytes 1572868
  147.7 2.4 %copy-start.22 = (bf16[1024,1024]{1,0:T(8,128)(2,1)S(1)}, bf16[1024,1024]{1,0:T(8,128)(2,1)}, u32[]{:S(2)}) copy-start(bf16[1024,1024]{1,0:T(8,128)(2,1)} %refs_8_.1) | copy-start | bytes 6291460
  150.1 2.4 %copy-start.2 = (bf16[16,16,1024]{2,1,0:T(8,128)(2,1)S(1)}, bf16[16,16,1024]{2,1,0:T(8,128)(2,1)}, u32[]{:S(2)}) copy-start(bf16[16,16,1024]{2,1,0:T(8,128)(2,1)} %param.11) | copy-start | bytes 1572868
  152.5 1.3 copy-start.24
  (1 other events, 0.7 us)
